TPU v7x, 32 devices: a whole 2x2x4 slice. The times are simulated.
32 devices in a mesh: rows: 8 (over y, x, core), cols: 4 (over z).
Axes of the slice: x: 2, y: 2, z: 4, core: 2. Of those that a mesh axis runs over, the one named last changes fastest.
Arguments:
- panel_t: float32 [256, 16384], P('cols', 'rows'), as said below
- trailing: float32 [16384, 1024], P('rows', 'cols'), may hold values from -6 to 6
- prev_lower_t: float32 [256, 16384], P('cols', 'rows'), may hold values from -6 to 6
- prev_upper: float32 [256, 1024], P(None, 'cols'), may hold values from -0.375 to 0.375
- leaf_picks: int32 [8, 256], P('rows'), may hold values from 0 to 2047, as said below
- merge_picks: int32 [7, 256], replicated, may hold values from 0 to 511, as said below
Outputs:
- lower_t: float32 [256, 16384], P('cols', 'rows')
- upper_left: float32 [256, 256], replicated
- upper_right: float32 [256, 1024], P(None, 'cols')
- updated: float32 [16384, 1024], P('rows', 'cols')
- gram: float32 [256, 256], P('cols')
Inputs may be any that keep to these rules, and one draw needn't show every extreme that they name: `leaf_picks`: each row lists 256 different row numbers within the 2048 rows of one index of rows. `merge_picks`: each row lists 256 different positions in a stack of two candidate lists. `panel_t`: the rows of the panel at the pivots form a strictly diagonally dominant block.
All inputs are finite; a program needn't handle non-finite values.
Results may differ from a plain program's by a relative error of at most 0.0003.
Values sent between devices are 32-bit elements; how exact they have to be, the bound alone decides.
A program may use at most 64 MiB of HBM per device.

v0:
```python
import jax
import jax.numpy as jnp
from jax import lax
from jax.sharding import PartitionSpec as P

full_precision = lax.Precision.HIGHEST


def from_partner(shard, axis, apart):
    return lax.ppermute(shard, axis, [(i, i ^ 1 << apart) for i in range(lax.axis_size(axis))])


def trace_pivots(merge_picks, row_devices):
    list_width = merge_picks.shape[1]
    leaf_group = jnp.zeros((list_width,), jnp.int32)
    leaf_slot = jnp.arange(list_width, dtype=jnp.int32)
    levels = row_devices.bit_length() - 1
    for section in reversed(range(levels)):
        offset_rows = row_devices - (row_devices >> section)
        position = merge_picks[offset_rows + leaf_group, leaf_slot]
        right_side = (position >= list_width).astype(jnp.int32)
        leaf_group = 2 * leaf_group + right_side
        leaf_slot = position - list_width * right_side
    return (leaf_group, leaf_slot)


def product(left_side, right_side):
    return jnp.dot(left_side, right_side, precision=full_precision)


def unit_lower_inverse(lower):
    order = lower.shape[0]
    identity = jnp.eye(order, dtype=jnp.float32)
    power = identity - lower
    result = identity + power
    covered = 1
    while covered < order - 1:
        power = product(power, power)
        result = product(result, identity + power)
        covered = 2 * covered + 1
    return result


def upper_inverse(upper):
    diagonal = jnp.diagonal(upper)
    scaled = upper / diagonal[:, None]
    unit_inverse = unit_lower_inverse(scaled.T).T
    return unit_inverse / diagonal[None, :]


def small_factor(matrix):
    order = matrix.shape[0]
    row_index = lax.broadcasted_iota(jnp.int32, (order, order), 0)
    col_index = lax.broadcasted_iota(jnp.int32, (order, order), 1)
    line_index = jnp.arange(order, dtype=jnp.int32)
    reduced = matrix
    for column_index in range(order - 1):
        pivot_line = jnp.sum(jnp.where(row_index == column_index, reduced, 0.0), 0)
        pivot_column = jnp.sum(jnp.where(col_index == column_index, reduced, 0.0), 1)
        pivot_value = jnp.sum(jnp.where(line_index == column_index, pivot_line, 0.0))
        factors = jnp.where(line_index > column_index, pivot_column / pivot_value, 0.0)
        below = row_index > column_index
        reduced = jnp.where(
            below & (col_index > column_index),
            reduced - factors[:, None] * pivot_line[None, :],
            reduced,
        )
        reduced = jnp.where(below & (col_index == column_index), factors[:, None], reduced)
    return (jnp.tril(reduced, -1) + jnp.eye(order, dtype=matrix.dtype), jnp.triu(reduced))


def factor(matrix):
    order = matrix.shape[0]
    if order <= 32:
        return small_factor(matrix)
    middle_index = order // 2
    lower_head, upper_head = factor(matrix[:middle_index, :middle_index])
    upper_side = product(unit_lower_inverse(lower_head), matrix[:middle_index, middle_index:])
    lower_side = product(matrix[middle_index:, :middle_index], upper_inverse(upper_head))
    schur_block = matrix[middle_index:, middle_index:] - product(lower_side, upper_side)
    lower_tail, upper_tail = factor(schur_block)
    zero_upper = jnp.zeros((middle_index, order - middle_index), matrix.dtype)
    zero_lower = jnp.zeros((order - middle_index, middle_index), matrix.dtype)
    lower_full = jnp.concatenate(
        [
            jnp.concatenate([lower_head, zero_upper], 1),
            jnp.concatenate([lower_side, lower_tail], 1),
        ],
        0,
    )
    upper_full = jnp.concatenate(
        [
            jnp.concatenate([upper_head, upper_side], 1),
            jnp.concatenate([zero_lower, upper_tail], 1),
        ],
        0,
    )
    return (lower_full, upper_full)


def contract_first(left_side, right_side):
    return lax.dot_general(
        left_side, right_side, (((0,), (0,)), ((), ())), precision=full_precision
    )


def contract_second(left_side, right_side):
    return lax.dot_general(
        left_side, right_side, (((1,), (1,)), ((), ())), precision=full_precision
    )


def body(panel_t, trailing, prev_lower_t, prev_upper, leaf_picks, merge_picks):
    slab_rows = panel_t.shape[0]
    rows_here = panel_t.shape[1]
    row_devices = lax.axis_size("rows")
    own_row = lax.axis_index("rows")
    own_column = lax.axis_index("cols")
    leaf_group, leaf_slot = trace_pivots(merge_picks, row_devices)
    owner_mask = leaf_group == own_row
    local_rows = jnp.take(leaf_picks[0], leaf_slot)
    middle = trailing
    middle = middle - contract_first(
        lax.all_gather(prev_lower_t, "cols", axis=0, tiled=True), prev_upper
    )
    panel_full = lax.all_gather(panel_t, "cols", axis=0, tiled=True)
    middle, panel_full = (middle, panel_full)
    candidates = jnp.take(panel_t, leaf_picks[0], axis=1)
    levels = row_devices.bit_length() - 1
    for section in range(levels):
        partner = from_partner(candidates, "rows", section)
        upper_half = own_row >> section & 1
        stacked = jnp.where(
            upper_half == 0,
            jnp.concatenate([candidates, partner], 1),
            jnp.concatenate([partner, candidates], 1),
        )
        merge_index = row_devices - (row_devices >> section) + (own_row >> section + 1)
        selection = lax.dynamic_index_in_dim(merge_picks, merge_index, 0, keepdims=False)
        candidates = jnp.take(stacked, selection, axis=1)
    block_t = lax.all_gather(candidates, "cols", axis=0, tiled=True)
    lower_left, upper_left = factor(block_t.T)
    inverse = upper_inverse(upper_left)
    chosen_rows = jnp.take(middle, local_rows, axis=0)
    pivot_trailing = lax.psum(jnp.where(owner_mask[:, None], chosen_rows, 0.0), "rows")
    upper_right = product(unit_lower_inverse(lower_left), pivot_trailing)
    lower_full = jnp.dot(inverse.T, panel_full, precision=full_precision)
    lower_tile = lax.dynamic_slice_in_dim(lower_full, own_column * slab_rows, slab_rows, 0)
    updated = middle - contract_first(lower_full, upper_right)
    gram_rows = contract_second(lower_tile, lower_full)
    gram = lax.psum(gram_rows, "rows") / (rows_here * row_devices)
    return (lower_tile, upper_left, upper_right, updated, gram)


def solution(mesh):
    return jax.shard_map(
        body,
        mesh=mesh,
        in_specs=(
            P("cols", "rows"),
            P("rows", "cols"),
            P("cols", "rows"),
            P(None, "cols"),
            P("rows", None),
            P(),
        ),
        out_specs=(P("cols", "rows"), P(), P(None, "cols"), P("rows", "cols"), P("cols", None)),
        check_vma=False,
    )
```

profile of v0, /device:TPU:0, one launch (start us, length us, event | category | flops | bytes accessed | tf_op | source)
XLA Modules:
  0.0 555.4 jit_solution(8430852429966456527)
XLA Ops:
  8.0 1.4 copy.115
  9.4 1.9 gather_fusion.9
  11.3 1.9 gather_fusion.10
  13.3 1.9 gather_fusion.11
  15.2 0.7 gather_fusion
  17.2 1.9 gather_fusion.12
  20.9 2.6 collective-permute-start.1
  23.5 4.2 collective-permute-done.1
  28.5 1.8 collective-permute-start.2
  30.3 3.6 collective-permute-done.2
  34.9 16.8 %all_gather.9 = f32[256,256]{1,0:T(8,128)S(1)} all-gather(f32[64,256]{1,0:T(8,128)S(1)} %select_bitcast_fusion.3), channel_id=1, replica_groups=mesh['rows'=8,'cols'=4] {'cols'}, dimensions={0}, use_global_device_ids=true | all-gather | bytes 327680 | tf_op jit(solution)/shard_map/all_gather | solution.py:141
  146.0 0.8 gather_fusion.2
  247.2 1.3 gather_fusion.4
  349.5 0.8 gather_fusion.6
  451.7 2.5 gather_fusion.8
  461.6 0.8 copy.218
  466.2 3.7 fusion.209
  470.0 2.7 fusion.217
  472.7 7.0 %convolution_subtract_fusion.1 = f32[2048,256]{1,0:T(8,128)} fusion(f32[2048,256]{1,0:T(8,128)} %param.9, f32[256,2048]{1,0:T(8,128)} %all-gather.5.cloned.1.call-done, f32[256,256]{1,0:T(8,128)S(1)} %copy-done), kind=kOutput, calls=%fused_computation.18 | convolution fusion | flops 1611137024 | bytes 6553600 | tf_op jit(solution)/shard_map/dot_general | solution.py:102
  479.7 3.2 gather_fusion.13
  482.9 1.8 select_select_fusion
  485.1 54.9 %all-reduce.17.cloned.1.call-done = (f32[256,256]{1,0:T(8,128)}, f32[64,256]{1,0:T(8,128)}) async-done(((f32[256,256]{1,0:T(8,128)}, f32[64,256]{1,0:T(8,128)}), (f32[256,256]{1,0:T(8,128)}, f32[64,256]{1,0:T(8,128)})) %all-reduce.17.cloned.1.call-update) | async-done | bytes 327696 | tf_op jit(solution)/shard_map/psum | solution.py:145
  540.0 1.3 fusion.216
  541.4 6.6 %convolution_subtract_fusion = f32[2048,256]{1,0:T(8,128)} fusion(f32[2048,256]{1,0:T(8,128)} %convolution_subtract_fusion.1, f32[256,2048]{1,0:T(8,128)S(1)} %fusion.209, f32[256,256]{1,0:T(8,128)S(1)} %fusion.216), kind=kOutput, calls=%fused_computation.17 | convolution fusion | flops 1611137024 | bytes 6553600 | tf_op jit(solution)/shard_map/dot_general | solution.py:102
  (1094 shorter events, 411.1 us)
Async XLA Ops:
  7.2 465.5 %copy-start = (f32[256,256]{1,0:T(8,128)S(1)}, f32[256,256]{1,0:T(8,128)}, u32[]{:S(2)}) copy-start(f32[256,256]{1,0:T(8,128)} %param.11) | copy-start | bytes 786436
  7.2 2.2 copy-start.3
  7.2 2.2 copy-start.1
  7.2 459.0 %all-gather.3.cloned.1.call-start = ((), (), s32[]{:S(2)}) async-start(), calls=%async_computation | async-start | bytes 2621440 | tf_op jit(solution)/shard_map/all_gather | solution.py:126
  7.9 464.8 %all-gather.5.cloned.1.call-start = ((), (), s32[]{:S(2)}) async-start(), calls=%async_computation.1 | async-start | bytes 2621440 | tf_op jit(solution)/shard_map/all_gather | solution.py:124
  9.4 5.8 %copy-start.2 = (s32[1,256]{1,0:T(1,128)S(1)}, s32[1,256]{1,0:T(1,128)}, u32[]{:S(2)}) copy-start(s32[1,256]{1,0:T(1,128)} %param.12) | copy-start | bytes 3076
  16.1 4.0 collective-permute-start
  16.6 523.4 %all-reduce.17.cloned.1.call-start = ((), (), s32[]{:S(2)}) async-start(), calls=%async_computation.2 | async-start | bytes 655360 | tf_op jit(solution)/shard_map/psum | solution.py:145
  20.9 6.7 %collective-permute-start.1 = (f32[64,256]{0,1:T(8,128)S(1)}, f32[64,256]{0,1:T(8,128)S(1)}, u32[]{:S(2)}, u32[]{:S(2)}) collective-permute-start(f32[64,256]{0,1:T(8,128)S(1)} %select_bitcast_fusion.1), channel_id=1, source_target_pairs={{0,8},{4,12},{8,0},{12,4},{16,24},{20,28},{24,16},{28,20},{1,9},{5... | collective-permute-start | bytes 196616 | tf_op jit(solution)/shard_map/ppermute | solution.py:10
  28.5 5.5 collective-permute-start.2
  470.0 9.7 %copy-start.4 = (f32[64,2048]{1,0:T(8,128)}, f32[64,2048]{1,0:T(8,128)S(1)}, u32[]{:S(2)}) copy-start(f32[64,2048]{1,0:T(8,128)S(1)} %constant_dynamic-slice_fusion) | copy-start | bytes 1572868
  541.4 6.7 %copy-start.5 = (f32[256,256]{1,0:T(8,128)}, f32[256,256]{1,0:T(8,128)S(1)}, u32[]{:S(2)}) copy-start(f32[256,256]{1,0:T(8,128)S(1)} %fusion.216) | copy-start | bytes 786436
  541.4 6.7 %copy-start.6 = (f32[64,256]{1,0:T(8,128)S(1)}, f32[64,256]{1,0:T(8,128)}, u32[]{:S(2)}) copy-start(f32[64,256]{1,0:T(8,128)} %get-tuple-element.511) | copy-start | bytes 196612
Sparse Core Ops, SparseCore 0:
  9.6 52.6 all-gather.2
  63.9 44.5 all-gather.4
  484.9 55.1 all-reduce.16
where the time goes:
time: 561 us; the launch traced here: 555 us
  other arithmetic  363 us (65%)
  waiting for transfers between devices  63.4 us (11%)
  matrix products  61.6 us (11%)
  local copies, waits for them, and re-layouts  28 us (5%)
  between operations  17.9 us (3%)
  blocking collectives  16.8 us (3%)
    select_n x248, other arithmetic, small_factor(): jnp.where(line_index > column_index, pivot_column / pivot_value, 0.0)  161 us
    reduce_sum x248, other arithmetic, small_factor(): jnp.sum(jnp.where(line_index == column_index, pivot_line, 0.0))  151 us
    psum x1, waiting for transfers between devices, body(): lax.psum(jnp.where(owner_mask[:, None], chosen_rows, 0.0), 'rows')  54.9 us
    reduce_sum x244, other arithmetic, small_factor(): jnp.sum(jnp.where(col_index == column_index, reduced, 0.0), 1)  45.1 us
    dot_general x178, matrix products, product(): return jnp.dot(left_side, right_side, precision=full_precision)  41.5 us
    all_gather x1, blocking collectives, body(): block_t = lax.all_gather(candidates, 'cols', axis=0, tiled=True)  16.8 us
    dot_general x2, matrix products, contract_first(): lax.dot_general(left_side, right_side, (((0,), (0,)), ((), ())), precisio...  13.6 us
  transfers between devices with their start and end apart: 6, of which 3 were waited for; matrix products, arithmetic and copies ran while one was open for 78% of the time, Pallas kernels for 0%

commit v1 on v0

v1 whole, which is shorter than its diff:
```python
import jax
import jax.numpy as jnp
from jax import lax
from jax.experimental import pallas as pl
from jax.experimental.pallas import tpu as pltpu
from jax.sharding import PartitionSpec as P

full_precision = lax.Precision.HIGH


def from_partner(shard, axis, apart):
    return lax.ppermute(shard, axis, [(i, i ^ 1 << apart) for i in range(lax.axis_size(axis))])


def trace_pivots(merge_picks, row_devices):
    list_width = merge_picks.shape[1]
    leaf_group = jnp.zeros((list_width,), jnp.int32)
    leaf_slot = jnp.arange(list_width, dtype=jnp.int32)
    levels = row_devices.bit_length() - 1
    for section in reversed(range(levels)):
        offset_rows = row_devices - (row_devices >> section)
        position = merge_picks[offset_rows + leaf_group, leaf_slot]
        right_side = (position >= list_width).astype(jnp.int32)
        leaf_group = 2 * leaf_group + right_side
        leaf_slot = position - list_width * right_side
    return (leaf_group, leaf_slot)


def product(left_side, right_side):
    return jnp.dot(left_side, right_side, precision=full_precision)


BLOCK = 32


def pieces(value):
    first = value.astype(jnp.bfloat16)
    rest = value - first.astype(jnp.float32)
    second = rest.astype(jnp.bfloat16)
    third = (rest - second.astype(jnp.float32)).astype(jnp.bfloat16)
    return first, second, third


def thin_product(left_t, right):
    l0, l1, l2 = pieces(left_t)
    r0, r1, r2 = pieces(right)
    left_stack = jnp.concatenate([l0, l0, l1, l1, l0, l2], 0)
    right_stack = jnp.concatenate([r0, r1, r0, r1, r2, r0], 0)
    return lax.dot_general(
        left_stack, right_stack, (((0,), (0,)), ((), ())), preferred_element_type=jnp.float32
    )


def eliminate(tiles):
    sub = lax.broadcasted_iota(jnp.int32, (8, 128), 0)
    groups = BLOCK // 8
    for k in range(BLOCK - 1):
        home, s = k // 8, k % 8
        for chain in tiles:
            row = [jnp.broadcast_to(t[s : s + 1, :], (8, 128)) for t in chain[home]]
            inverse = 1.0 / row[0]
            for g in range(home, groups):
                if g == home and s == 7:
                    continue
                scaled = chain[g][0] * inverse
                if g == home:
                    scaled = jnp.where(sub > s, scaled, 0.0)
                factor = jnp.broadcast_to(scaled[:, k : k + 1], (8, 128))
                chain[g] = [t - factor * r for t, r in zip(chain[g], row)]
    return tiles


def lu_stage(stage, order, w, x, u_ref, linv_ref, uinvt_ref):
    groups = BLOCK // 8
    start = pl.multiple_of(stage * BLOCK, BLOCK)
    rows = pl.ds(start, BLOCK)
    back = lax.rem(order - start, order)
    spare = order // 128
    lane = lax.broadcasted_iota(jnp.int32, (BLOCK, order), 1)
    sub = lax.broadcasted_iota(jnp.int32, (BLOCK, order), 0)
    eye8 = lax.broadcasted_iota(jnp.int32, (8, 128), 1) - lax.broadcasted_iota(
        jnp.int32, (8, 128), 0
    )
    chains = []
    for ref in (w, x):
        turned = pltpu.roll(ref[rows, :], back, 1)
        chain = []
        for g in range(groups):
            part = [turned[8 * g : 8 * g + 8, 128 * t : 128 * t + 128] for t in range(spare)]
            part.append(jnp.where(eye8 == 8 * g, 1.0, 0.0))
            chain.append(part)
        chains.append(chain)
    chains = eliminate(chains)
    full, joined, diagonal = [], [], []
    for chain in chains:
        main = jnp.concatenate(
            [jnp.concatenate([chain[g][t] for g in range(groups)], 0) for t in range(spare)], 1
        )
        extra = jnp.concatenate([chain[g][spare] for g in range(groups)], 0)
        extra = jnp.concatenate([extra] + [jnp.zeros((BLOCK, 128), jnp.float32)] * (spare - 1), 1)
        pivot = jnp.sum(jnp.where(lane == sub, main, 0.0), 1, keepdims=True)
        mixed = jnp.where(lane < BLOCK, extra, main)
        full.append(pltpu.roll(main, start, 1))
        joined.append(pltpu.roll(mixed, start, 1))
        diagonal.append(pivot)
    u_ref[rows, :] = jnp.where(lane >= sub + start, full[0], 0.0)
    reached = lane < start + BLOCK
    inverse_w = 1.0 / diagonal[0]
    inverse_x = 1.0 / diagonal[1]
    linv_ref[rows, :] = jnp.where(reached, joined[0], 0.0)
    uinvt_ref[rows, :] = jnp.where(reached, joined[1] * inverse_x, 0.0)
    lower = jnp.where(reached, 0.0, full[1] * inverse_x)
    upper = jnp.where(reached, 0.0, full[0] * inverse_w)
    cols = lax.broadcasted_iota(jnp.int32, (order, order), 1)
    inside = (cols >= start) & (cols < start + BLOCK)
    w[...] = jnp.where(inside, 0.0, w[...]) - thin_product(lower, joined[0])
    x[...] = jnp.where(inside, 0.0, x[...]) - thin_product(upper, joined[1])


def lu_kernel(a_ref, at_ref, u_ref, linv_ref, uinvt_ref, w, x):
    order = a_ref.shape[0]
    w[...] = a_ref[...]
    x[...] = at_ref[...]

    @pl.loop(0, order // BLOCK)
    def _(stage):
        lu_stage(stage, order, w, x, u_ref, linv_ref, uinvt_ref)


def factor(block, block_t):
    order = block.shape[0]
    shape = jax.ShapeDtypeStruct((order, order), jnp.float32)
    return pl.pallas_call(
        lu_kernel,
        out_shape=[shape] * 3,
        in_specs=[pl.BlockSpec(memory_space=pltpu.VMEM)] * 2,
        out_specs=[pl.BlockSpec(memory_space=pltpu.VMEM)] * 3,
        scratch_shapes=[pltpu.VMEM((order, order), jnp.float32)] * 2,
        compiler_params=pltpu.CompilerParams(vmem_limit_bytes=32 * 1024 * 1024),
        name="block_factors",
    )(block, block_t)


def contract_first(left_side, right_side):
    return lax.dot_general(
        left_side, right_side, (((0,), (0,)), ((), ())), precision=full_precision
    )


def contract_second(left_side, right_side):
    return lax.dot_general(
        left_side, right_side, (((1,), (1,)), ((), ())), precision=full_precision
    )


def body(panel_t, trailing, prev_lower_t, prev_upper, leaf_picks, merge_picks):
    slab_rows = panel_t.shape[0]
    rows_here = panel_t.shape[1]
    row_devices = lax.axis_size("rows")
    own_row = lax.axis_index("rows")
    own_column = lax.axis_index("cols")
    leaf_group, leaf_slot = trace_pivots(merge_picks, row_devices)
    owner_mask = leaf_group == own_row
    local_rows = jnp.take(leaf_picks[0], leaf_slot)
    middle = trailing
    middle = middle - contract_first(
        lax.all_gather(prev_lower_t, "cols", axis=0, tiled=True), prev_upper
    )
    panel_full = lax.all_gather(panel_t, "cols", axis=0, tiled=True)
    candidates = jnp.take(panel_t, leaf_picks[0], axis=1)
    levels = row_devices.bit_length() - 1
    for section in range(levels):
        partner = from_partner(candidates, "rows", section)
        upper_half = own_row >> section & 1
        stacked = jnp.where(
            upper_half == 0,
            jnp.concatenate([candidates, partner], 1),
            jnp.concatenate([partner, candidates], 1),
        )
        merge_index = row_devices - (row_devices >> section) + (own_row >> section + 1)
        selection = lax.dynamic_index_in_dim(merge_picks, merge_index, 0, keepdims=False)
        candidates = jnp.take(stacked, selection, axis=1)
    block_t = lax.all_gather(candidates, "cols", axis=0, tiled=True)
    upper_left, lower_inverse, inverse_t = factor(block_t.T, block_t)
    chosen_rows = jnp.take(middle, local_rows, axis=0)
    pivot_trailing = lax.psum(jnp.where(owner_mask[:, None], chosen_rows, 0.0), "rows")
    upper_right = product(lower_inverse, pivot_trailing)
    lower_full = product(inverse_t, panel_full)
    lower_tile = lax.dynamic_slice_in_dim(lower_full, own_column * slab_rows, slab_rows, 0)
    updated = middle - contract_first(lower_full, upper_right)
    gram_rows = contract_second(lower_tile, lower_full)
    gram = lax.psum(gram_rows, "rows") / (rows_here * row_devices)
    return (lower_tile, upper_left, upper_right, updated, gram)


def solution(mesh):
    return jax.shard_map(
        body,
        mesh=mesh,
        in_specs=(
            P("cols", "rows"),
            P("rows", "cols"),
            P("cols", "rows"),
            P(None, "cols"),
            P("rows", None),
            P(),
        ),
        out_specs=(P("cols", "rows"), P(), P(None, "cols"), P("rows", "cols"), P("cols", None)),
        check_vma=False,
    )
```

time: 561 us -> 184 us (0.33); the launches traced: 555 us -> 184 us
  other arithmetic: 363 us -> 2 us
  matrix products: 61.6 us -> 15.8 us
  waiting for transfers between devices: 63.4 us -> 91.4 us
  Pallas kernels: 0 us -> 24.3 us
  local copies, waits for them, and re-layouts: 28 us -> 14.8 us
    reduce_sum x493 -> x0, other arithmetic: 196 us -> none  [the longest x248 151 us: small_factor(): jnp.sum(jnp.where(line_index == column_index, pivot_line, 0.0))]
    select_n x255 -> x0, other arithmetic: 161 us -> none  [the longest x248 161 us: small_factor(): jnp.where(line_index > column_index, pivot_column / pivot_value, 0.0)]
    dot_general x178 -> x2, matrix products: 41.5 us -> 3.85 us  [product(): return jnp.dot(left_side, right_side, precision=full_precision)]
    all_gather x1, waiting for transfers between devices: 0.01 us -> 29.4 us  [body(): lax.all_gather(prev_lower_t, 'cols', axis=0, tiled=True)]
    pallas_call x0 -> x1, Pallas kernels: none -> 24.3 us  [factor(): pl.pallas_call(lu_kernel, out_shape=[shape] * 3, in_specs=[pl.BlockSpec(m...]
    gather x8 -> x0, local copies, waits for them, and re-layouts: 8.32 us -> none  [upper_inverse(): diagonal = jnp.diagonal(upper)]
  transfers between devices with their start and end apart: 6 -> 6, of which waited for: 3 -> 4; matrix products, arithmetic and copies ran while one was open for 78% -> 9% of each run, Pallas kernels for 0% -> 13%
where the time goes in v1:
time: 184 us
  waiting for transfers between devices  91.4 us (50%)
  Pallas kernels  24.3 us (13%)
  blocking collectives  16.7 us (9%)
  matrix products  15.8 us (9%)
  local copies, waits for them, and re-layouts  14.8 us (8%)
  between operations  14.1 us (8%)
  starting transfers between devices  5.03 us (3%)
  other arithmetic  2 us (1%)
    psum x1, waiting for transfers between devices, body(): lax.psum(jnp.where(owner_mask[:, None], chosen_rows, 0.0), 'rows')  53.5 us
    all_gather x1, waiting for transfers between devices, body(): lax.all_gather(prev_lower_t, 'cols', axis=0, tiled=True)  29.4 us
    pallas_call x1, Pallas kernels, factor(): pl.pallas_call(lu_kernel, out_shape=[shape] * 3, in_specs=[pl.BlockSpec(m...  24.3 us
    all_gather x1, blocking collectives, body(): block_t = lax.all_gather(candidates, 'cols', axis=0, tiled=True)  16.7 us
    dot_general x2, matrix products, contract_first(): lax.dot_general(left_side, right_side, (((0,), (0,)), ((), ())), precisio...  10.2 us
    ppermute x3, waiting for transfers between devices, from_partner(): lax.ppermute(shard, axis, [(i, i ^ 1 << apart) for i in range(lax.axis_si...  7.81 us
    gather x3, local copies, waits for them, and re-layouts, trace_pivots(): position = merge_picks[offset_rows + leaf_group, leaf_slot]  5.69 us
    ppermute x3, starting transfers between devices, from_partner(): lax.ppermute(shard, axis, [(i, i ^ 1 << apart) for i in range(lax.axis_si...  4.92 us
  transfers between devices with their start and end apart: 6, of which 4 were waited for; matrix products, arithmetic and copies ran while one was open for 9% of the time, Pallas kernels for 13%

profile of v1, /device:TPU:0, one launch (start us, length us, event | category | flops | bytes accessed | tf_op | source)
XLA Modules:
  0.0 184.1 jit_solution(7481099788168977409)
XLA Ops:
  8.0 1.4 copy.14
  9.4 1.9 %gather_fusion.1 = s32[256]{0:T(256)S(1)} fusion(s32[7,256]{1,0:T(8,128)S(1)} %copy-done.1, s32[256]{0:T(256)S(1)} %copy-done.3), kind=kCustom, calls=%fused_computation.4 | custom fusion | bytes 4096 | tf_op jit(solution)/shard_map/gather | solution.py:22
  11.3 1.9 %gather_fusion.2 = s32[256]{0:T(256)S(1)} fusion(s32[7,256]{1,0:T(8,128)S(1)} %copy-done.1, s32[256]{0:T(256)S(1)} %bitcast.38), kind=kCustom, calls=%fused_computation.5 | custom fusion | bytes 4096 | tf_op jit(solution)/shard_map/gather | solution.py:22
  13.3 1.9 %gather_fusion.3 = s32[256]{0:T(256)S(1)} fusion(s32[7,256]{1,0:T(8,128)S(1)} %copy-done.1, s32[256]{0:T(256)S(1)} %bitcast.37), kind=kCustom, calls=%fused_computation.6 | custom fusion | bytes 4096 | tf_op jit(solution)/shard_map/gather | solution.py:22
  15.2 0.7 gather_fusion
  16.7 1.9 %gather_fusion.4 = s32[256]{0:T(256)S(1)} fusion(s32[256]{0:T(256)S(1)} %bitcast.36, s32[1024]{0:T(1024)S(1)} %pad_clamp_fusion.1), kind=kCustom, calls=%fused_computation.7 | custom fusion | bytes 3072 | tf_op jit(solution)/shard_map/jit(_take)/gather | solution.py:164
  18.8 0.7 gather_fusion.6
  19.7 2.6 %collective-permute-start.1 = (f32[64,256]{0,1:T(8,128)S(1)}, f32[64,256]{0,1:T(8,128)S(1)}, u32[]{:S(2)}, u32[]{:S(2)}) collective-permute-start(f32[64,256]{0,1:T(8,128)S(1)} %select_bitcast_fusion.1), channel_id=1, source_target_pairs={{0,8},{4,12},{8,0},{12,4},{16,24},{20,28},{24,16},{28,20},{1,9},{5... | collective-permute-start | bytes 196616 | tf_op jit(solution)/shard_map/ppermute | solution.py:12
  22.2 4.2 %collective-permute-done.1 = f32[64,256]{0,1:T(8,128)S(1)} collective-permute-done((f32[64,256]{0,1:T(8,128)S(1)}, f32[64,256]{0,1:T(8,128)S(1)}, u32[]{:S(2)}, u32[]{:S(2)}) %collective-permute-start.1) | collective-permute-done | bytes 65568 | tf_op jit(solution)/shard_map/ppermute | solution.py:12
  26.4 0.7 gather_fusion.7
  27.2 1.8 collective-permute-start.2
  29.1 3.7 %collective-permute-done.2 = f32[64,256]{0,1:T(8,128)S(1)} collective-permute-done((f32[64,256]{0,1:T(8,128)S(1)}, f32[64,256]{0,1:T(8,128)S(1)}, u32[]{:S(2)}, u32[]{:S(2)}) %collective-permute-start.2) | collective-permute-done | bytes 65568 | tf_op jit(solution)/shard_map/ppermute | solution.py:12
  32.8 0.7 gather_fusion.8
  33.6 16.7 %all_gather.9.at_ref = f32[256,256]{1,0:T(8,128)S(1)} all-gather(f32[64,256]{1,0:T(8,128)S(1)} %select_bitcast_fusion.3), channel_id=1, replica_groups=mesh['rows'=8,'cols'=4] {'cols'}, dimensions={0}, use_global_device_ids=true | all-gather | bytes 327680 | tf_op jit(solution)/shard_map/all_gather | solution.py:183
  50.4 24.3 %block_factors.1 = (f32[256,256]{1,0:T(8,128)}, f32[256,256]{1,0:T(8,128)S(1)}, f32[256,256]{1,0:T(8,128)S(1)}) custom-call(f32[256,256]{1,0:T(8,128)S(1)} %copy.16.a_ref, f32[256,256]{1,0:T(8,128)S(1)} %all_gather.9.at_ref), custom_call_target="tpu_custom_call" | custom-call | tf_op jit(solution)/shard_map/block_factors/pallas_call | solution.py:133
  74.8 2.6 %fusion.14 = f32[256,2048]{1,0:T(8,128)S(1)} fusion(f32[256,256]{1,0:T(8,128)S(1)} %get-tuple-element.9, f32[256,2048]{1,0:T(8,128)} %all-gather.3.cloned.1.call-done), kind=kOutput, calls=%fused_computation.70 | convolution fusion | flops 805306368 | bytes 4456448 | tf_op jit(solution)/shard_map/dot_general | solution.py:30
  77.5 1.7 fusion.16
  79.2 29.4 %all-gather.5.cloned.1.call-done = f32[256,2048]{1,0:T(8,128)} async-done(((f32[64,2048]{1,0:T(8,128)}), f32[256,2048]{1,0:T(8,128)}) %all-gather.5.cloned.1.call-update) | async-done | bytes 2097168 | tf_op jit(solution)/shard_map/all_gather | solution.py:167
  108.6 5.4 %convolution_subtract_fusion.1 = f32[2048,256]{1,0:T(8,128)} fusion(f32[2048,256]{1,0:T(8,128)} %param.9, f32[256,2048]{1,0:T(8,128)} %all-gather.5.cloned.1.call-done, f32[256,256]{1,0:T(8,128)S(1)} %copy-done), kind=kOutput, calls=%fused_computation.10 | convolution fusion | flops 805830656 | bytes 6553600 | tf_op jit(solution)/shard_map/dot_general | solution.py:145
  113.9 2.6 %gather_fusion.5 = f32[256,256]{1,0:T(8,128)S(1)} fusion(f32[2048,256]{1,0:T(8,128)} %convolution_subtract_fusion.1, s32[1024]{0:T(1024)S(1)} %pad_clamp_fusion), kind=kCustom, calls=%fused_computation.8 | custom fusion | bytes 525312 | tf_op jit(solution)/shard_map/jit(_take)/gather | solution.py:185
  116.5 0.8 select_select_fusion
  117.3 53.5 %all-reduce.3.cloned.1.call-done = (f32[256,256]{1,0:T(8,128)}, f32[64,256]{1,0:T(8,128)}) async-done(((f32[256,256]{1,0:T(8,128)}, f32[64,256]{1,0:T(8,128)}), (f32[256,256]{1,0:T(8,128)}, f32[64,256]{1,0:T(8,128)})) %all-reduce.3.cloned.1.call-update) | async-done | bytes 327696 | tf_op jit(solution)/shard_map/psum | solution.py:186
  170.9 1.2 fusion.15
  172.1 4.9 %convolution_subtract_fusion = f32[2048,256]{1,0:T(8,128)} fusion(f32[2048,256]{1,0:T(8,128)} %convolution_subtract_fusion.1, f32[256,2048]{1,0:T(8,128)S(1)} %fusion.14, f32[256,256]{1,0:T(8,128)S(1)} %fusion.15), kind=kOutput, calls=%fused_computation.9 | convolution fusion | flops 805830656 | bytes 6553600 | tf_op jit(solution)/shard_map/dot_general | solution.py:145
  (52 shorter events, 2.8 us)
Async XLA Ops:
  7.2 101.4 %copy-start = (f32[256,256]{1,0:T(8,128)S(1)}, f32[256,256]{1,0:T(8,128)}, u32[]{:S(2)}) copy-start(f32[256,256]{1,0:T(8,128)} %param.11) | copy-start | bytes 786436
  7.2 2.2 %copy-start.3 = (s32[256]{0:T(256)S(1)}, s32[256]{0:T(256)}, u32[]{:S(2)}) copy-start(s32[256]{0:T(256)} %constant.155) | copy-start | bytes 3076
  7.2 2.2 %copy-start.1 = (s32[7,256]{1,0:T(8,128)S(1)}, s32[7,256]{1,0:T(8,128)}, u32[]{:S(2)}) copy-start(s32[7,256]{1,0:T(8,128)} %param.13) | copy-start | bytes 21508
  7.2 67.5 %all-gather.3.cloned.1.call-start = ((), (), s32[]{:S(2)}) async-start(), calls=%async_computation | async-start | bytes 2621440 | tf_op jit(solution)/shard_map/all_gather | solution.py:169
  7.9 100.6 %all-gather.5.cloned.1.call-start = ((), (), s32[]{:S(2)}) async-start(), calls=%async_computation.1 | async-start | bytes 2621440 | tf_op jit(solution)/shard_map/all_gather | solution.py:167
  9.4 5.8 %copy-start.2 = (s32[1,256]{1,0:T(1,128)S(1)}, s32[1,256]{1,0:T(1,128)}, u32[]{:S(2)}) copy-start(s32[1,256]{1,0:T(1,128)} %param.12) | copy-start | bytes 3076
  16.1 2.7 %collective-permute-start = (f32[64,256]{0,1:T(8,128)S(1)}, f32[64,256]{0,1:T(8,128)S(1)}, u32[]{:S(2)}, u32[]{:S(2)}) collective-permute-start(f32[64,256]{0,1:T(8,128)S(1)} %select_bitcast_fusion.2), channel_id=1, source_target_pairs={{0,4},{4,0},{8,12},{12,8},{16,20},{20,16},{24,28},{28,24},{1,5},{5... | collective-permute-start | bytes 196616 | tf_op jit(solution)/shard_map/ppermute | solution.py:12
  16.6 154.3 %all-reduce.3.cloned.1.call-start = ((), (), s32[]{:S(2)}) async-start(), calls=%async_computation.2 | async-start | bytes 655360 | tf_op jit(solution)/shard_map/psum | solution.py:186
  19.7 6.7 %collective-permute-start.1 = (f32[64,256]{0,1:T(8,128)S(1)}, f32[64,256]{0,1:T(8,128)S(1)}, u32[]{:S(2)}, u32[]{:S(2)}) collective-permute-start(f32[64,256]{0,1:T(8,128)S(1)} %select_bitcast_fusion.1), channel_id=1, source_target_pairs={{0,8},{4,12},{8,0},{12,4},{16,24},{20,28},{24,16},{28,20},{1,9},{5... | collective-permute-start | bytes 196616 | tf_op jit(solution)/shard_map/ppermute | solution.py:12
  27.2 5.5 %collective-permute-start.2 = (f32[64,256]{0,1:T(8,128)S(1)}, f32[64,256]{0,1:T(8,128)S(1)}, u32[]{:S(2)}, u32[]{:S(2)}) collective-permute-start(f32[64,256]{0,1:T(8,128)S(1)} %select_bitcast_fusion), channel_id=1, source_target_pairs={{0,16},{4,20},{8,24},{12,28},{16,0},{20,4},{24,8},{28,12},{1,17},{... | collective-permute-start | bytes 196616 | tf_op jit(solution)/shard_map/ppermute | solution.py:12
  77.4 36.5 %copy-start.4 = (f32[64,2048]{1,0:T(8,128)}, f32[64,2048]{1,0:T(8,128)S(1)}, u32[]{:S(2)}) copy-start(f32[64,2048]{1,0:T(8,128)S(1)} %constant_dynamic-slice_fusion) | copy-start | bytes 1572868
  172.1 4.9 %copy-start.5 = (f32[256,256]{1,0:T(8,128)}, f32[256,256]{1,0:T(8,128)S(1)}, u32[]{:S(2)}) copy-start(f32[256,256]{1,0:T(8,128)S(1)} %fusion.15) | copy-start | bytes 786436
  172.1 4.9 %copy-start.6 = (f32[64,256]{1,0:T(8,128)S(1)}, f32[64,256]{1,0:T(8,128)}, u32[]{:S(2)}) copy-start(f32[64,256]{1,0:T(8,128)} %get-tuple-element.13) | copy-start | bytes 196612
Sparse Core Ops, SparseCore 0:
  9.6 52.7 all-gather.2
  63.9 44.5 all-gather.4
  117.5 53.3 all-reduce.2

commit v2 on v1

v2 whole, which is shorter than its diff:
```python
import functools
import jax
import jax.numpy as jnp
from jax import lax
from jax.experimental import pallas as pl
from jax.experimental.pallas import tpu as pltpu
from jax.sharding import PartitionSpec as P

MESH = pl.DeviceIdType.MESH
PIECES = 8

BLOCK = 32


def pieces(value):
    first = value.astype(jnp.bfloat16)
    rest = value - first.astype(jnp.float32)
    second = rest.astype(jnp.bfloat16)
    third = (rest - second.astype(jnp.float32)).astype(jnp.bfloat16)
    return first, second, third


def thin_product(left_t, right):
    l0, l1, l2 = pieces(left_t)
    r0, r1, r2 = pieces(right)
    left_stack = jnp.concatenate([l0, l0, l1, l1, l0, l2], 0)
    right_stack = jnp.concatenate([r0, r1, r0, r1, r2, r0], 0)
    return lax.dot_general(
        left_stack, right_stack, (((0,), (0,)), ((), ())), preferred_element_type=jnp.float32
    )


def eliminate(tiles):
    sub = lax.broadcasted_iota(jnp.int32, (8, 128), 0)
    groups = BLOCK // 8
    for k in range(BLOCK - 1):
        home, s = k // 8, k % 8
        for chain in tiles:
            row = [jnp.broadcast_to(t[s : s + 1, :], (8, 128)) for t in chain[home]]
            inverse = 1.0 / row[0]
            for g in range(home, groups):
                if g == home and s == 7:
                    continue
                scaled = chain[g][0] * inverse
                if g == home:
                    scaled = jnp.where(sub > s, scaled, 0.0)
                factor = jnp.broadcast_to(scaled[:, k : k + 1], (8, 128))
                chain[g] = [t - factor * r for t, r in zip(chain[g], row)]
    return tiles


def lu_stage(stage, order, w, x, u_ref, linv_ref, uinvt_ref):
    groups = BLOCK // 8
    start = pl.multiple_of(stage * BLOCK, BLOCK)
    rows = pl.ds(start, BLOCK)
    back = lax.rem(order - start, order)
    spare = order // 128
    lane = lax.broadcasted_iota(jnp.int32, (BLOCK, order), 1)
    sub = lax.broadcasted_iota(jnp.int32, (BLOCK, order), 0)
    eye8 = lax.broadcasted_iota(jnp.int32, (8, 128), 1) - lax.broadcasted_iota(
        jnp.int32, (8, 128), 0
    )
    chains = []
    for ref in (w, x):
        turned = pltpu.roll(ref[rows, :], back, 1)
        chain = []
        for g in range(groups):
            part = [turned[8 * g : 8 * g + 8, 128 * t : 128 * t + 128] for t in range(spare)]
            part.append(jnp.where(eye8 == 8 * g, 1.0, 0.0))
            chain.append(part)
        chains.append(chain)
    chains = eliminate(chains)
    full, joined, diagonal = [], [], []
    for chain in chains:
        main = jnp.concatenate(
            [jnp.concatenate([chain[g][t] for g in range(groups)], 0) for t in range(spare)], 1
        )
        extra = jnp.concatenate([chain[g][spare] for g in range(groups)], 0)
        extra = jnp.concatenate([extra] + [jnp.zeros((BLOCK, 128), jnp.float32)] * (spare - 1), 1)
        pivot = jnp.sum(jnp.where(lane == sub, main, 0.0), 1, keepdims=True)
        mixed = jnp.where(lane < BLOCK, extra, main)
        full.append(pltpu.roll(main, start, 1))
        joined.append(pltpu.roll(mixed, start, 1))
        diagonal.append(pivot)
    u_ref[rows, :] = jnp.where(lane >= sub + start, full[0], 0.0)
    reached = lane < start + BLOCK
    inverse_w = 1.0 / diagonal[0]
    inverse_x = 1.0 / diagonal[1]
    linv_ref[rows, :] = jnp.where(reached, joined[0], 0.0)
    uinvt_ref[rows, :] = jnp.where(reached, joined[1] * inverse_x, 0.0)
    lower = jnp.where(reached, 0.0, full[1] * inverse_x)
    upper = jnp.where(reached, 0.0, full[0] * inverse_w)
    cols = lax.broadcasted_iota(jnp.int32, (order, order), 1)
    inside = (cols >= start) & (cols < start + BLOCK)
    w[...] = jnp.where(inside, 0.0, w[...]) - thin_product(lower, joined[0])
    x[...] = jnp.where(inside, 0.0, x[...]) - thin_product(upper, joined[1])


def halves(value):
    first = value.astype(jnp.bfloat16)
    return first, (value - first.astype(jnp.float32)).astype(jnp.bfloat16)


def product(left, right, left_dim=1, right_dim=0):
    dims = (((left_dim,), (right_dim,)), ((), ()))
    a0, a1 = halves(left)
    b0, b1 = halves(right)
    dot = functools.partial(
        lax.dot_general, dimension_numbers=dims, preferred_element_type=jnp.float32
    )
    return dot(a0, b0) + (dot(a0, b1) + dot(a1, b0))


def trace_rows(merge_ref, leaf_ref, row_devices, own_row):
    width = merge_ref.shape[1]
    lane = lax.broadcasted_iota(jnp.int32, (width, width), 1)
    slot = lax.broadcasted_iota(jnp.int32, (width, 1), 0)
    group = jnp.zeros((width, 1), jnp.int32)

    def look_up(table):
        found = jnp.where(lane == slot, table.astype(jnp.float32), 0.0)
        return jnp.sum(found, 1, keepdims=True).astype(jnp.int32)

    for section in reversed(range(row_devices.bit_length() - 1)):
        offset = row_devices - (row_devices >> section)
        table = jnp.broadcast_to(merge_ref[offset : offset + 1, :], (width, width))
        for g in range(1, row_devices >> (section + 1)):
            line = merge_ref[offset + g : offset + g + 1, :]
            table = jnp.where(group == g, line, table)
        position = look_up(table)
        right_side = (position >= width).astype(jnp.int32)
        group = 2 * group + right_side
        slot = position - width * right_side
    local = look_up(jnp.broadcast_to(leaf_ref[...], (width, width)))
    return jnp.where(group == own_row, local, -1)


def step_kernel(
    row_devices,
    col_devices,
    panel_ref,
    trailing_ref,
    prev_ref,
    prev_upper_ref,
    leaf_ref,
    merge_ref,
    lower_ref,
    u_ref,
    right_ref,
    updated_ref,
    gram_ref,
    tall,
    picked,
    picked_in,
    block,
    trail,
    trail_in,
    trail_all,
    w,
    x,
    linv,
    uinvt,
    lower_full,
    gram_in,
    tall_send,
    tall_recv,
    row_send,
    row_recv,
    zone_send,
    zone_recv,
):
    slab, rows_here = panel_ref.shape
    order = merge_ref.shape[1]
    trail_cols = trailing_ref.shape[1]
    share = order // row_devices
    span = rows_here // PIECES
    own_row = lax.axis_index("rows")
    own_col = lax.axis_index("cols")

    barrier = pltpu.get_barrier_semaphore()

    @pl.loop(1, row_devices)
    def _(d):
        pl.semaphore_signal(
            barrier,
            inc=1,
            device_id={"rows": lax.rem(own_row + d, row_devices)},
            device_id_type=MESH,
        )

    @pl.loop(1, col_devices)
    def _(d):
        pl.semaphore_signal(
            barrier,
            inc=1,
            device_id={"cols": lax.rem(own_col + d, col_devices)},
            device_id_type=MESH,
        )

    for q in range(PIECES):
        part = slice(q * span, (q + 1) * span)
        tall[q, own_col, :slab, :] = panel_ref[:, part]
        tall[q, own_col, slab:, :] = prev_ref[:, part]

    pl.semaphore_wait(barrier, row_devices + col_devices - 2)

    def tall_copy(q, source, way, to):
        place = tall.at[q, source]
        return pltpu.make_async_remote_copy(
            src_ref=place,
            dst_ref=place,
            send_sem=tall_send.at[way, source, q],
            recv_sem=tall_recv.at[source, q],
            device_id={"cols": to},
            device_id_type=MESH,
        )

    def tick(time):
        @pl.loop(0, col_devices)
        def _(hop):
            q = time - hop

            @pl.when((q >= 0) & (q < PIECES))
            def _():
                up = own_col - hop
                down = own_col + hop

                @pl.when((hop > 0) & (up >= 0))
                def _():
                    tall_copy(q, up, 0, own_col - 1).wait_recv()

                @pl.when((up >= 0) & (own_col < col_devices - 1))
                def _():
                    tall_copy(q, up, 0, own_col + 1).start()

                @pl.when((hop > 0) & (down < col_devices))
                def _():
                    tall_copy(q, down, 1, own_col + 1).wait_recv()

                @pl.when((down < col_devices) & (own_col > 0))
                def _():
                    tall_copy(q, down, 1, own_col - 1).start()

    def share_of(d):
        return pl.ds(pl.multiple_of(lax.rem(own_row + d, row_devices) * share, share), share)

    def row_copy(kind, d, src, dst):
        return pltpu.make_async_remote_copy(
            src_ref=src,
            dst_ref=dst,
            send_sem=row_send.at[kind, d],
            recv_sem=row_recv.at[kind, d],
            device_id={"rows": lax.rem(own_row + d, row_devices)},
            device_id_type=MESH,
        )

    def picked_copy(d):
        return row_copy(0, d, picked.at[share_of(d), :], picked_in.at[d])

    def block_copy(d):
        return row_copy(1, d, block.at[own_row], block.at[own_row])

    def trail_copy(d):
        return row_copy(2, d, trail.at[share_of(d), :], trail_in.at[d])

    def trail_out_copy(d):
        return row_copy(3, d, trail_all.at[own_row], trail_all.at[own_row])

    def gram_copy(d):
        return row_copy(4, d, gram_in.at[0], gram_in.at[d])

    def zone_copy(d):
        return pltpu.make_async_remote_copy(
            src_ref=block.at[own_row, own_col],
            dst_ref=block.at[own_row, own_col],
            send_sem=zone_send.at[d],
            recv_sem=zone_recv.at[d],
            device_id={"cols": lax.rem(own_col + d, col_devices)},
            device_id_type=MESH,
        )

    def start_all(copy, count):
        @pl.loop(1, count)
        def _(d):
            copy(d).start()

    def land_all(copy, count):
        @pl.loop(1, count)
        def _(d):
            copy(d).wait_recv()

    def sent_all(copy, count):
        @pl.loop(1, count)
        def _(d):
            copy(d).wait_send()

    target = trace_rows(merge_ref, leaf_ref, row_devices, own_row)
    lane = lax.broadcasted_iota(jnp.int32, (order, span), 1)

    def one_hot(q):
        return jnp.where(lane + q * span == target, 1.0, 0.0).astype(jnp.bfloat16)

    total = jnp.zeros((order, 128), jnp.float32)
    for q in range(PIECES):
        stack = tall[q, own_col]
        if 2 * slab < 128:
            stack = jnp.concatenate([stack, jnp.zeros((128 - 2 * slab, span), jnp.float32)], 0)
        found = lax.dot_general(
            one_hot(q),
            jnp.concatenate(pieces(stack), 0),
            (((1,), (1,)), ((), ())),
            preferred_element_type=jnp.float32,
        )
        total = total + (found[:, :128] + found[:, 128:256] + found[:, 256:])
    picked[...] = total
    start_all(picked_copy, row_devices)
    tick(0)

    total = jnp.zeros((order, trail_cols), jnp.float32)
    for q in range(PIECES):
        chosen = one_hot(q)
        for part in pieces(trailing_ref[q * span : (q + 1) * span, :]):
            total = total + jnp.dot(chosen, part, preferred_element_type=jnp.float32)
    trail[...] = total

    land_all(picked_copy, row_devices)
    total = picked[share_of(0), :]
    for d in range(1, row_devices):
        total = total + picked_in[d]
    block[own_row, own_col] = total
    start_all(zone_copy, col_devices)
    land_all(zone_copy, col_devices)
    start_all(block_copy, row_devices)
    start_all(trail_copy, row_devices)
    land_all(block_copy, row_devices)
    tick(1)

    def gathered(first):
        parts = []
        for z in range(col_devices):
            parts.append(block[:, z].reshape(order, 128)[:, first : first + slab])
        return jnp.concatenate(parts, 1)

    matrix = gathered(0)
    w[...] = matrix
    x[...] = matrix.T

    def stages(first, last):
        @pl.loop(first, last)
        def _(stage):
            lu_stage(stage, order, w, x, u_ref, linv, uinvt)

    count = order // BLOCK
    stages(0, count // 4)
    land_all(trail_copy, row_devices)
    total = trail[share_of(0), :]
    for d in range(1, row_devices):
        total = total + trail_in[d]
    trail_all[own_row] = total
    start_all(trail_out_copy, row_devices)
    tick(2)
    stages(count // 4, 5 * count // 8)
    tick(3)
    stages(5 * count // 8, count)

    @pl.loop(4, col_devices + 1)
    def _(time):
        tick(time)

    land_all(trail_out_copy, row_devices)
    chosen = trail_all[...].reshape(order, trail_cols)
    chosen = chosen - product(gathered(slab), prev_upper_ref[...])
    right_ref[...] = product(linv[...], chosen)
    gram_in[0] = jnp.zeros((slab, order), jnp.float32)

    @pl.loop(0, PIECES)
    def _(q):
        here = pl.ds(pl.multiple_of(q * span, span), span)
        panel_full = tall[q, :, :slab, :].reshape(order, span)
        prev_full = tall[q, :, slab:, :].reshape(order, span)
        lower = product(uinvt[...], panel_full)
        lower_full[...] = lower
        tile = lower_full[pl.ds(pl.multiple_of(own_col * slab, slab), slab), :]
        lower_ref[:, here] = tile
        gram_in[0] += product(tile, lower, 1, 1)
        middle = trailing_ref[here, :] - product(prev_full, prev_upper_ref[...], 0, 0)
        updated_ref[here, :] = middle - product(lower, right_ref[...], 0, 0)
        tick(q + col_devices + 1)

    start_all(gram_copy, row_devices)
    sent_all(picked_copy, row_devices)
    sent_all(zone_copy, col_devices)
    sent_all(block_copy, row_devices)
    sent_all(trail_copy, row_devices)
    sent_all(trail_out_copy, row_devices)

    @pl.loop(0, PIECES)
    def _(q):
        @pl.loop(0, col_devices)
        def _(source):
            @pl.when((source <= own_col) & (own_col < col_devices - 1))
            def _():
                tall_copy(q, source, 0, own_col + 1).wait_send()

            @pl.when((source >= own_col) & (own_col > 0))
            def _():
                tall_copy(q, source, 1, own_col - 1).wait_send()

    land_all(gram_copy, row_devices)
    total = gram_in[0]
    for d in range(1, row_devices):
        total = total + gram_in[d]
    gram_ref[...] = total / (rows_here * row_devices)
    sent_all(gram_copy, row_devices)


def body(row_devices, col_devices, panel_t, trailing, prev_lower_t, prev_upper, leaf, merge):
    slab, rows_here = panel_t.shape
    order = merge.shape[1]
    trail_cols = trailing.shape[1]
    share = order // row_devices
    span = rows_here // PIECES
    real = jnp.float32
    square = pltpu.VMEM((order, order), real)
    vmem = pl.BlockSpec(memory_space=pltpu.VMEM)
    dma = pltpu.SemaphoreType.DMA
    return pl.pallas_call(
        functools.partial(step_kernel, row_devices, col_devices),
        out_shape=[
            jax.ShapeDtypeStruct((slab, rows_here), real),
            jax.ShapeDtypeStruct((order, order), real),
            jax.ShapeDtypeStruct((order, trail_cols), real),
            jax.ShapeDtypeStruct((rows_here, trail_cols), real),
            jax.ShapeDtypeStruct((slab, order), real),
        ],
        in_specs=[vmem] * 6,
        out_specs=[vmem] * 5,
        scratch_shapes=[
            pltpu.VMEM((PIECES, col_devices, 2 * slab, span), real),
            pltpu.VMEM((order, 128), real),
            pltpu.VMEM((row_devices, share, 128), real),
            pltpu.VMEM((row_devices, col_devices, share, 128), real),
            pltpu.VMEM((order, trail_cols), real),
            pltpu.VMEM((row_devices, share, trail_cols), real),
            pltpu.VMEM((row_devices, share, trail_cols), real),
            square,
            square,
            square,
            square,
            pltpu.VMEM((order, span), real),
            pltpu.VMEM((row_devices, slab, order), real),
            dma((2, col_devices, PIECES)),
            dma((col_devices, PIECES)),
            dma((5, row_devices)),
            dma((5, row_devices)),
            dma((col_devices,)),
            dma((col_devices,)),
        ],
        compiler_params=pltpu.CompilerParams(
            collective_id=0, has_side_effects=True, vmem_limit_bytes=48 * 1024 * 1024
        ),
        name="panel_step",
    )(panel_t, trailing, prev_lower_t, prev_upper, leaf, merge)


def solution(mesh):
    return jax.shard_map(
        functools.partial(body, mesh.shape["rows"], mesh.shape["cols"]),
        mesh=mesh,
        in_specs=(
            P("cols", "rows"),
            P("rows", "cols"),
            P("cols", "rows"),
            P(None, "cols"),
            P("rows", None),
            P(),
        ),
        out_specs=(P("cols", "rows"), P(), P(None, "cols"), P("rows", "cols"), P("cols", None)),
        check_vma=False,
    )
```

time: 184 us -> 114 us (0.62)
  waiting for transfers between devices: 91.4 us -> 0 us
  Pallas kernels: 24.3 us -> 104 us
  blocking collectives: 16.7 us -> 0 us
  matrix products: 15.8 us -> 0 us
  between operations: 14.1 us -> 0.66 us
  local copies, waits for them, and re-layouts: 14.8 us -> 8.55 us
  starting transfers between devices: 5.03 us -> 0 us
  other arithmetic: 2 us -> 0 us
    pallas_call x1, Pallas kernels: 24.3 us -> 104 us  [body(): pl.pallas_call(functools.partial(step_kernel, row_devices, col_devices),...]
    psum x1 -> x0, waiting for transfers between devices: 53.5 us -> none  [body(): lax.psum(jnp.where(owner_mask[:, None], chosen_rows, 0.0), 'rows')]
    all_gather x2 -> x0, waiting for transfers between devices: 29.4 us -> none  [the longest x1 29.4 us: body(): lax.all_gather(prev_lower_t, 'cols', axis=0, tiled=True)]
    all_gather x1 -> x0, blocking collectives: 16.7 us -> none  [body(): block_t = lax.all_gather(candidates, 'cols', axis=0, tiled=True)]
    dot_general x5 -> x0, matrix products: 15.8 us -> none  [the longest x2 10.2 us: contract_first(): lax.dot_general(left_side, right_side, (((0,), (0,)), ((), ())), precisio...]
    gather x10 -> x0, local copies, waits for them, and re-layouts: 13.2 us -> none  [the longest x3 5.69 us: trace_pivots(): position = merge_picks[offset_rows + leaf_group, leaf_slot]]
    ppermute x3 -> x0, waiting for transfers between devices: 7.81 us -> none  [from_partner(): lax.ppermute(shard, axis, [(i, i ^ 1 << apart) for i in range(lax.axis_si...]
    unnamed x15, local copies, waits for them, and re-layouts: 1.41 us -> 8.55 us
  transfers between devices with their start and end apart: 6 -> 0, of which waited for: 4 -> 0; matrix products, arithmetic and copies ran while one was open for 9% -> 0% of each run, Pallas kernels for 13% -> 0%
where the time goes in v2:
time: 114 us; the launch traced here: 113 us
  Pallas kernels  104 us (91%)
  local copies, waits for them, and re-layouts  8.55 us (8%)
    pallas_call x1, Pallas kernels, body(): pl.pallas_call(functools.partial(step_kernel, row_devices, col_devices),...  104 us
    unnamed x15, local copies, waits for them, and re-layouts  8.55 us

profile of v2, /device:TPU:0, one launch (start us, length us, event | category | flops | bytes accessed | tf_op | source)
XLA Modules:
  0.0 113.2 jit_solution(14286075392193443845)
XLA Ops:
  0.6 0.0 copy-start
  0.6 1.0 copy-done
  1.7 0.0 copy-start.1
  1.7 1.0 copy-done.1
  2.7 0.0 copy-start.2
  2.7 0.9 copy-done.2
  3.7 0.0 copy-start.3
  3.7 0.7 copy-done.3
  4.4 0.0 copy-start.4
  4.4 0.7 copy-done.4
  5.0 104.0 %panel_step.1 = (f32[64,2048]{1,0:T(8,128)S(1)}, f32[256,256]{1,0:T(8,128)S(1)}, f32[256,256]{1,0:T(8,128)S(1)}, f32[2048,256]{1,0:T(8,128)S(1)}, f32[64,256]{1,0:T(8,128)S(1)}) custom-call(f32[64,2048]{1,0:T(8,128)S(1)} %copy-done, f32[2048,256]{1,0:T(8,128)} %trailing_ref.1, f32[64,2048]{1,0:T(8,128)S(1)} %copy-done.1, f32[256,256]{1,0:T(8,128)S(1)} %copy-done.2, ...), custom_call_target="tpu_custom_call" | custom-call | tf_op jit(solution)/shard_map/panel_step/pallas_call | solution.py:427
  109.0 0.8 copy.16
  109.8 0.7 copy.17
  110.5 0.7 copy.18
  111.2 1.3 %copy.19 = f32[2048,256]{1,0:T(8,128)} copy(f32[2048,256]{1,0:T(8,128)S(1)} %get-tuple-element.13) | data formatting | bytes 4194304
  112.5 0.6 copy.20
Async XLA Ops:
  0.6 1.0 copy-start
  1.7 1.0 copy-start.1
  2.7 0.9 copy-start.2
  3.7 0.7 copy-start.3
  4.4 0.7 copy-start.4

commit v3 on v2

--- a/solution.py
+++ b/solution.py
@@ -138,16 +138,24 @@
 def step_kernel(
     row_devices,
     col_devices,
-    panel_ref,
+    panel_hbm,
+    trailing_hbm,
+    prev_hbm,
+    prev_upper_hbm,
+    leaf_hbm,
+    merge_hbm,
+    lower_hbm,
+    u_hbm,
+    right_hbm,
+    updated_hbm,
+    gram_hbm,
     trailing_ref,
-    prev_ref,
     prev_upper_ref,
     leaf_ref,
     merge_ref,
     lower_ref,
     u_ref,
     right_ref,
-    updated_ref,
     gram_ref,
     tall,
     picked,
@@ -168,8 +176,12 @@
     row_recv,
     zone_send,
     zone_recv,
+    own_sem,
+    in_sem,
+    piece_sem,
+    out_sem,
 ):
-    slab, rows_here = panel_ref.shape
+    slab, rows_here = panel_hbm.shape
     order = merge_ref.shape[1]
     trail_cols = trailing_ref.shape[1]
     share = order // row_devices
@@ -197,11 +209,32 @@
             device_id_type=MESH,
         )
 
+    own_copies = []
     for q in range(PIECES):
-        part = slice(q * span, (q + 1) * span)
-        tall[q, own_col, :slab, :] = panel_ref[:, part]
-        tall[q, own_col, slab:, :] = prev_ref[:, part]
-
+        part = pl.ds(q * span, span)
+        for kind, (source, rows) in enumerate(
+            ((panel_hbm, pl.ds(0, slab)), (prev_hbm, pl.ds(slab, slab)))
+        ):
+            own_copies.append(
+                pltpu.make_async_copy(
+                    source.at[:, part], tall.at[q, own_col, rows, :], own_sem.at[kind, q]
+                )
+            )
+    loads = [
+        pltpu.make_async_copy(source, place, in_sem.at[i])
+        for i, (source, place) in enumerate(
+            (
+                (merge_hbm, merge_ref),
+                (leaf_hbm, leaf_ref),
+                (trailing_hbm, trailing_ref),
+                (prev_upper_hbm, prev_upper_ref),
+            )
+        )
+    ]
+    for copy in loads[:2] + own_copies + loads[2:]:
+        copy.start()
+    for copy in own_copies:
+        copy.wait()
     pl.semaphore_wait(barrier, row_devices + col_devices - 2)
 
     def tall_copy(q, source, way, to):
@@ -215,31 +248,28 @@
             device_id_type=MESH,
         )
 
-    def tick(time):
-        @pl.loop(0, col_devices)
-        def _(hop):
-            q = time - hop
-
-            @pl.when((q >= 0) & (q < PIECES))
+    def step(hop, q):
+        up = own_col - hop
+        down = own_col + hop
+        if hop > 0:
+
+            @pl.when(up >= 0)
             def _():
-                up = own_col - hop
-                down = own_col + hop
-
-                @pl.when((hop > 0) & (up >= 0))
-                def _():
-                    tall_copy(q, up, 0, own_col - 1).wait_recv()
-
-                @pl.when((up >= 0) & (own_col < col_devices - 1))
-                def _():
-                    tall_copy(q, up, 0, own_col + 1).start()
-
-                @pl.when((hop > 0) & (down < col_devices))
-                def _():
-                    tall_copy(q, down, 1, own_col + 1).wait_recv()
-
-                @pl.when((down < col_devices) & (own_col > 0))
-                def _():
-                    tall_copy(q, down, 1, own_col - 1).start()
+                tall_copy(q, up, 0, own_col - 1).wait_recv()
+
+        @pl.when((up >= 0) & (own_col < col_devices - 1))
+        def _():
+            tall_copy(q, up, 0, own_col + 1).start()
+
+        if hop > 0:
+
+            @pl.when(down < col_devices)
+            def _():
+                tall_copy(q, down, 1, own_col + 1).wait_recv()
+
+        @pl.when((down < col_devices) & (own_col > 0))
+        def _():
+            tall_copy(q, down, 1, own_col - 1).start()
 
     def share_of(d):
         return pl.ds(pl.multiple_of(lax.rem(own_row + d, row_devices) * share, share), share)
@@ -294,6 +324,10 @@
         def _(d):
             copy(d).wait_send()
 
+    for q in range(2):
+        step(0, q)
+    loads[0].wait()
+    loads[1].wait()
     target = trace_rows(merge_ref, leaf_ref, row_devices, own_row)
     lane = lax.broadcasted_iota(jnp.int32, (order, span), 1)
 
@@ -314,7 +348,8 @@
         total = total + (found[:, :128] + found[:, 128:256] + found[:, 256:])
     picked[...] = total
     start_all(picked_copy, row_devices)
-    tick(0)
+    loads[2].wait()
+    loads[3].wait()
 
     total = jnp.zeros((order, trail_cols), jnp.float32)
     for q in range(PIECES):
@@ -332,8 +367,9 @@
     land_all(zone_copy, col_devices)
     start_all(block_copy, row_devices)
     start_all(trail_copy, row_devices)
+    for q in range(2, PIECES):
+        step(0, q)
     land_all(block_copy, row_devices)
-    tick(1)
 
     def gathered(first):
         parts = []
@@ -345,36 +381,50 @@
     w[...] = matrix
     x[...] = matrix.T
 
-    def stages(first, last):
-        @pl.loop(first, last)
-        def _(stage):
-            lu_stage(stage, order, w, x, u_ref, linv, uinvt)
-
     count = order // BLOCK
-    stages(0, count // 4)
-    land_all(trail_copy, row_devices)
-    total = trail[share_of(0), :]
-    for d in range(1, row_devices):
-        total = total + trail_in[d]
-    trail_all[own_row] = total
-    start_all(trail_out_copy, row_devices)
-    tick(2)
-    stages(count // 4, 5 * count // 8)
-    tick(3)
-    stages(5 * count // 8, count)
-
-    @pl.loop(4, col_devices + 1)
-    def _(time):
-        tick(time)
+
+    @pl.loop(0, count)
+    def _(stage):
+        lu_stage(stage, order, w, x, u_ref, linv, uinvt)
+        for part in range(PIECES // count):
+            step(1, stage * (PIECES // count) + part)
+
+        @pl.when(stage == 2)
+        def _():
+            land_all(trail_copy, row_devices)
+            total = trail[share_of(0), :]
+            for d in range(1, row_devices):
+                total = total + trail_in[d]
+            trail_all[own_row] = total
+            start_all(trail_out_copy, row_devices)
 
     land_all(trail_out_copy, row_devices)
     chosen = trail_all[...].reshape(order, trail_cols)
     chosen = chosen - product(gathered(slab), prev_upper_ref[...])
     right_ref[...] = product(linv[...], chosen)
     gram_in[0] = jnp.zeros((slab, order), jnp.float32)
+    u_copy = pltpu.make_async_copy(u_ref, u_hbm, out_sem.at[0])
+    right_copy = pltpu.make_async_copy(right_ref, right_hbm, out_sem.at[1])
+    u_copy.start()
+    right_copy.start()
+    for hop in range(2, col_devices - 1):
+
+        @pl.loop(0, PIECES)
+        def _(q):
+            step(hop, q)
+
+    def piece_copies(q):
+        here = pl.ds(pl.multiple_of(q * span, span), span)
+        return (
+            pltpu.make_async_copy(lower_ref.at[:, here], lower_hbm.at[:, here], piece_sem.at[0, q]),
+            pltpu.make_async_copy(
+                trailing_ref.at[here, :], updated_hbm.at[here, :], piece_sem.at[1, q]
+            ),
+        )
 
     @pl.loop(0, PIECES)
     def _(q):
+        step(col_devices - 1, q)
         here = pl.ds(pl.multiple_of(q * span, span), span)
         panel_full = tall[q, :, :slab, :].reshape(order, span)
         prev_full = tall[q, :, slab:, :].reshape(order, span)
@@ -383,11 +433,16 @@
         tile = lower_full[pl.ds(pl.multiple_of(own_col * slab, slab), slab), :]
         lower_ref[:, here] = tile
         gram_in[0] += product(tile, lower, 1, 1)
+
+        @pl.when(q == PIECES - 1)
+        def _():
+            start_all(gram_copy, row_devices)
+
         middle = trailing_ref[here, :] - product(prev_full, prev_upper_ref[...], 0, 0)
-        updated_ref[here, :] = middle - product(lower, right_ref[...], 0, 0)
-        tick(q + col_devices + 1)
-
-    start_all(gram_copy, row_devices)
+        trailing_ref[here, :] = middle - product(lower, right_ref[...], 0, 0)
+        for copy in piece_copies(q):
+            copy.start()
+
     sent_all(picked_copy, row_devices)
     sent_all(zone_copy, col_devices)
     sent_all(block_copy, row_devices)
@@ -411,7 +466,35 @@
     for d in range(1, row_devices):
         total = total + gram_in[d]
     gram_ref[...] = total / (rows_here * row_devices)
+    last = pltpu.make_async_copy(gram_ref, gram_hbm, out_sem.at[2])
+    last.start()
     sent_all(gram_copy, row_devices)
+
+    @pl.loop(0, PIECES)
+    def _(q):
+        for copy in piece_copies(q):
+            copy.wait()
+
+    u_copy.wait()
+    right_copy.wait()
+    last.wait()
+
+
+def place_kernel(*refs):
+    sources, places, sem = refs[:5], refs[5:10], refs[10]
+    copies = []
+    for source, place in zip(sources, places):
+        height = source.shape[0]
+        parts = 4 if height >= 1024 else 1
+        for part in range(parts):
+            rows = pl.ds(part * (height // parts), height // parts)
+            copies.append(
+                pltpu.make_async_copy(source.at[rows, :], place.at[rows, :], sem.at[len(copies)])
+            )
+    for copy in copies:
+        copy.start()
+    for copy in copies:
+        copy.wait()
 
 
 def body(row_devices, col_devices, panel_t, trailing, prev_lower_t, prev_upper, leaf, merge):
@@ -422,20 +505,29 @@
     span = rows_here // PIECES
     real = jnp.float32
     square = pltpu.VMEM((order, order), real)
-    vmem = pl.BlockSpec(memory_space=pltpu.VMEM)
+    anywhere = pl.BlockSpec(memory_space=pl.ANY)
     dma = pltpu.SemaphoreType.DMA
-    return pl.pallas_call(
+    shapes = [
+        jax.ShapeDtypeStruct((slab, rows_here), real),
+        jax.ShapeDtypeStruct((order, order), real),
+        jax.ShapeDtypeStruct((order, trail_cols), real),
+        jax.ShapeDtypeStruct((rows_here, trail_cols), real),
+        jax.ShapeDtypeStruct((slab, order), real),
+    ]
+    results = pl.pallas_call(
         functools.partial(step_kernel, row_devices, col_devices),
-        out_shape=[
-            jax.ShapeDtypeStruct((slab, rows_here), real),
-            jax.ShapeDtypeStruct((order, order), real),
-            jax.ShapeDtypeStruct((order, trail_cols), real),
-            jax.ShapeDtypeStruct((rows_here, trail_cols), real),
-            jax.ShapeDtypeStruct((slab, order), real),
-        ],
-        in_specs=[vmem] * 6,
-        out_specs=[vmem] * 5,
+        out_shape=shapes,
+        in_specs=[anywhere] * 6,
+        out_specs=[anywhere] * 5,
         scratch_shapes=[
+            pltpu.VMEM((rows_here, trail_cols), real),
+            pltpu.VMEM((order, trail_cols), real),
+            pltpu.VMEM((1, order), jnp.int32),
+            pltpu.VMEM(merge.shape, jnp.int32),
+            pltpu.VMEM((slab, rows_here), real),
+            square,
+            pltpu.VMEM((order, trail_cols), real),
+            pltpu.VMEM((slab, order), real),
             pltpu.VMEM((PIECES, col_devices, 2 * slab, span), real),
             pltpu.VMEM((order, 128), real),
             pltpu.VMEM((row_devices, share, 128), real),
@@ -455,12 +547,25 @@
             dma((5, row_devices)),
             dma((col_devices,)),
             dma((col_devices,)),
+            dma((2, PIECES)),
+            dma((4,)),
+            dma((2, PIECES)),
+            dma((3,)),
         ],
         compiler_params=pltpu.CompilerParams(
-            collective_id=0, has_side_effects=True, vmem_limit_bytes=48 * 1024 * 1024
+            collective_id=0, has_side_effects=True, vmem_limit_bytes=56 * 1024 * 1024
         ),
         name="panel_step",
     )(panel_t, trailing, prev_lower_t, prev_upper, leaf, merge)
+    return pl.pallas_call(
+        place_kernel,
+        out_shape=shapes,
+        in_specs=[anywhere] * 5,
+        out_specs=[anywhere] * 5,
+        scratch_shapes=[dma((8,))],
+        compiler_params=pltpu.CompilerParams(vmem_limit_bytes=56 * 1024 * 1024),
+        name="place_outputs",
+    )(*results)
 
 
 def solution(mesh):

time: 114 us -> 185 us (1.62)
  Pallas kernels: 104 us -> 185 us
  local copies, waits for them, and re-layouts: 8.55 us -> 0 us
    pallas_call x0 -> x1, Pallas kernels: none -> 98.5 us  [body(): pl.pallas_call(place_kernel, out_shape=shapes, in_specs=[anywhere] * 5, o...]
    pallas_call x1, Pallas kernels: 104 us -> 86.1 us  [body(): pl.pallas_call(functools.partial(step_kernel, row_devices, col_devices),...]
    unnamed x15 -> x0, local copies, waits for them, and re-layouts: 8.55 us -> none
where the time goes in v3:
time: 185 us
  Pallas kernels  185 us (100%)
    pallas_call x1, Pallas kernels, body(): pl.pallas_call(place_kernel, out_shape=shapes, in_specs=[anywhere] * 5, o...  98.5 us
    pallas_call x1, Pallas kernels, body(): pl.pallas_call(functools.partial(step_kernel, row_devices, col_devices),...  86.1 us

profile of v3, /device:TPU:0, one launch (start us, length us, event | category | flops | bytes accessed | tf_op | source)
XLA Modules:
  0.0 185.2 jit_solution(13452528257879861295)
XLA Ops:
  0.6 86.1 %panel_step.1 = (f32[64,2048]{1,0:T(8,128)}, f32[256,256]{1,0:T(8,128)}, f32[256,256]{1,0:T(8,128)}, f32[2048,256]{1,0:T(8,128)}, f32[64,256]{1,0:T(8,128)}) custom-call(f32[64,2048]{1,0:T(8,128)} %panel_hbm.1, f32[2048,256]{1,0:T(8,128)} %trailing_hbm.1, f32[64,2048]{1,0:T(8,128)} %prev_hbm.1, f32[256,256]{1,0:T(8,128)} %prev_upper_hbm.1, ...), custom_call_target="tpu_custom_call" | custom-call | tf_op jit(solution)/shard_map/panel_step/pallas_call | solution.py:517
  86.7 98.5 %place_outputs.1 = (f32[64,2048]{1,0:T(8,128)}, f32[256,256]{1,0:T(8,128)}, f32[256,256]{1,0:T(8,128)}, f32[2048,256]{1,0:T(8,128)}, f32[64,256]{1,0:T(8,128)}) custom-call(f32[64,2048]{1,0:T(8,128)} %get-tuple-element.10.refs_0_, f32[256,256]{1,0:T(8,128)} %get-tuple-element.11.refs_1_, f32[256,256]{1,0:T(8,128)} %get-tuple-element.12.refs_2_, ...), custom_call_target="tpu_custom_call" | custom-call | tf_op jit(solution)/shard_map/place_outputs/pallas_call | solution.py:560

commit v4 on v3

--- a/solution.py
+++ b/solution.py
@@ -8,6 +8,7 @@
 
 MESH = pl.DeviceIdType.MESH
 PIECES = 8
+HALF = PIECES // 2
 
 BLOCK = 32
 
@@ -185,7 +186,7 @@
     order = merge_ref.shape[1]
     trail_cols = trailing_ref.shape[1]
     share = order // row_devices
-    span = rows_here // PIECES
+    span = rows_here // HALF
     own_row = lax.axis_index("rows")
     own_col = lax.axis_index("cols")
 
@@ -211,15 +212,11 @@
 
     own_copies = []
     for q in range(PIECES):
-        part = pl.ds(q * span, span)
-        for kind, (source, rows) in enumerate(
-            ((panel_hbm, pl.ds(0, slab)), (prev_hbm, pl.ds(slab, slab)))
-        ):
-            own_copies.append(
-                pltpu.make_async_copy(
-                    source.at[:, part], tall.at[q, own_col, rows, :], own_sem.at[kind, q]
-                )
-            )
+        source = panel_hbm if q < HALF else prev_hbm
+        part = pl.ds(q % HALF * span, span)
+        own_copies.append(
+            pltpu.make_async_copy(source.at[:, part], tall.at[q, own_col], own_sem.at[q])
+        )
     loads = [
         pltpu.make_async_copy(source, place, in_sem.at[i])
         for i, (source, place) in enumerate(
@@ -324,7 +321,7 @@
         def _(d):
             copy(d).wait_send()
 
-    for q in range(2):
+    for q in range(HALF):
         step(0, q)
     loads[0].wait()
     loads[1].wait()
@@ -335,8 +332,8 @@
         return jnp.where(lane + q * span == target, 1.0, 0.0).astype(jnp.bfloat16)
 
     total = jnp.zeros((order, 128), jnp.float32)
-    for q in range(PIECES):
-        stack = tall[q, own_col]
+    for q in range(HALF):
+        stack = jnp.concatenate([tall[q, own_col], tall[q + HALF, own_col]], 0)
         if 2 * slab < 128:
             stack = jnp.concatenate([stack, jnp.zeros((128 - 2 * slab, span), jnp.float32)], 0)
         found = lax.dot_general(
@@ -352,7 +349,7 @@
     loads[3].wait()
 
     total = jnp.zeros((order, trail_cols), jnp.float32)
-    for q in range(PIECES):
+    for q in range(HALF):
         chosen = one_hot(q)
         for part in pieces(trailing_ref[q * span : (q + 1) * span, :]):
             total = total + jnp.dot(chosen, part, preferred_element_type=jnp.float32)
@@ -367,7 +364,7 @@
     land_all(zone_copy, col_devices)
     start_all(block_copy, row_devices)
     start_all(trail_copy, row_devices)
-    for q in range(2, PIECES):
+    for q in range(HALF, PIECES):
         step(0, q)
     land_all(block_copy, row_devices)
 
@@ -422,26 +419,43 @@
             ),
         )
 
-    @pl.loop(0, PIECES)
+    @pl.loop(0, HALF)
     def _(q):
         step(col_devices - 1, q)
         here = pl.ds(pl.multiple_of(q * span, span), span)
-        panel_full = tall[q, :, :slab, :].reshape(order, span)
-        prev_full = tall[q, :, slab:, :].reshape(order, span)
-        lower = product(uinvt[...], panel_full)
-        lower_full[...] = lower
-        tile = lower_full[pl.ds(pl.multiple_of(own_col * slab, slab), slab), :]
+        lower = product(uinvt[...], tall[q].reshape(order, span))
+        lower_full[q] = lower
+        tile = lower_full[q, pl.ds(pl.multiple_of(own_col * slab, slab), slab), :]
         lower_ref[:, here] = tile
+        piece_copies(q)[0].start()
         gram_in[0] += product(tile, lower, 1, 1)
 
-        @pl.when(q == PIECES - 1)
+        @pl.when(q == HALF - 1)
         def _():
             start_all(gram_copy, row_devices)
 
-        middle = trailing_ref[here, :] - product(prev_full, prev_upper_ref[...], 0, 0)
-        trailing_ref[here, :] = middle - product(lower, right_ref[...], 0, 0)
-        for copy in piece_copies(q):
-            copy.start()
+        trailing_ref[here, :] = trailing_ref[here, :] - product(lower, right_ref[...], 0, 0)
+
+    last = pltpu.make_async_copy(gram_ref, gram_hbm, out_sem.at[2])
+
+    @pl.loop(0, HALF)
+    def _(q):
+        @pl.when(q == HALF - 1)
+        def _():
+            land_all(gram_copy, row_devices)
+            total = gram_in[0]
+            for d in range(1, row_devices):
+                total = total + gram_in[d]
+            gram_ref[...] = total / (rows_here * row_devices)
+            last.start()
+
+        step(col_devices - 1, q + HALF)
+        here = pl.ds(pl.multiple_of(q * span, span), span)
+        prev_full = tall[q + HALF].reshape(order, span)
+        trailing_ref[here, :] = trailing_ref[here, :] - product(
+            prev_full, prev_upper_ref[...], 0, 0
+        )
+        piece_copies(q)[1].start()
 
     sent_all(picked_copy, row_devices)
     sent_all(zone_copy, col_devices)
@@ -461,16 +475,9 @@
             def _():
                 tall_copy(q, source, 1, own_col - 1).wait_send()
 
-    land_all(gram_copy, row_devices)
-    total = gram_in[0]
-    for d in range(1, row_devices):
-        total = total + gram_in[d]
-    gram_ref[...] = total / (rows_here * row_devices)
-    last = pltpu.make_async_copy(gram_ref, gram_hbm, out_sem.at[2])
-    last.start()
     sent_all(gram_copy, row_devices)
 
-    @pl.loop(0, PIECES)
+    @pl.loop(0, HALF)
     def _(q):
         for copy in piece_copies(q):
             copy.wait()
@@ -481,19 +488,23 @@
 
 
 def place_kernel(*refs):
-    sources, places, sem = refs[:5], refs[5:10], refs[10]
-    copies = []
-    for source, place in zip(sources, places):
+    sources, places, held, in_sem, out_sem = refs[:5], refs[5:10], refs[10:15], refs[15], refs[16]
+    arrivals, departures = [], []
+    for source, place, middle in zip(sources, places, held):
         height = source.shape[0]
         parts = 4 if height >= 1024 else 1
         for part in range(parts):
             rows = pl.ds(part * (height // parts), height // parts)
-            copies.append(
-                pltpu.make_async_copy(source.at[rows, :], place.at[rows, :], sem.at[len(copies)])
-            )
-    for copy in copies:
+            here = middle.at[rows, :]
+            index = len(arrivals)
+            arrivals.append(pltpu.make_async_copy(source.at[rows, :], here, in_sem.at[index]))
+            departures.append(pltpu.make_async_copy(here, place.at[rows, :], out_sem.at[index]))
+    for copy in arrivals:
         copy.start()
-    for copy in copies:
+    for arrival, departure in zip(arrivals, departures):
+        arrival.wait()
+        departure.start()
+    for copy in departures:
         copy.wait()
 
 
@@ -502,7 +513,7 @@
     order = merge.shape[1]
     trail_cols = trailing.shape[1]
     share = order // row_devices
-    span = rows_here // PIECES
+    span = rows_here // HALF
     real = jnp.float32
     square = pltpu.VMEM((order, order), real)
     anywhere = pl.BlockSpec(memory_space=pl.ANY)
@@ -528,7 +539,7 @@
             square,
             pltpu.VMEM((order, trail_cols), real),
             pltpu.VMEM((slab, order), real),
-            pltpu.VMEM((PIECES, col_devices, 2 * slab, span), real),
+            pltpu.VMEM((PIECES, col_devices, slab, span), real),
             pltpu.VMEM((order, 128), real),
             pltpu.VMEM((row_devices, share, 128), real),
             pltpu.VMEM((row_devices, col_devices, share, 128), real),
@@ -539,7 +550,7 @@
             square,
             square,
             square,
-            pltpu.VMEM((order, span), real),
+            pltpu.VMEM((HALF, order, span), real),
             pltpu.VMEM((row_devices, slab, order), real),
             dma((2, col_devices, PIECES)),
             dma((col_devices, PIECES)),
@@ -547,9 +558,9 @@
             dma((5, row_devices)),
             dma((col_devices,)),
             dma((col_devices,)),
-            dma((2, PIECES)),
+            dma((PIECES,)),
             dma((4,)),
-            dma((2, PIECES)),
+            dma((2, HALF)),
             dma((3,)),
         ],
         compiler_params=pltpu.CompilerParams(
@@ -562,7 +573,7 @@
         out_shape=shapes,
         in_specs=[anywhere] * 5,
         out_specs=[anywhere] * 5,
-        scratch_shapes=[dma((8,))],
+        scratch_shapes=[pltpu.VMEM(shape.shape, real) for shape in shapes] + [dma((8,))] * 2,
         compiler_params=pltpu.CompilerParams(vmem_limit_bytes=56 * 1024 * 1024),
         name="place_outputs",
     )(*results)

time: 185 us -> 85.6 us (0.46)
  Pallas kernels: 185 us -> 84.8 us
    pallas_call x1, Pallas kernels: 98.5 us -> 2.85 us  [body(): pl.pallas_call(place_kernel, out_shape=shapes, in_specs=[anywhere] * 5, o...]
    pallas_call x1, Pallas kernels: 86.1 us -> 82 us  [body(): pl.pallas_call(functools.partial(step_kernel, row_devices, col_devices),...]
where the time goes in v4:
time: 85.6 us; the launch traced here: 85.4 us
  Pallas kernels  84.8 us (99%)
    pallas_call x1, Pallas kernels, body(): pl.pallas_call(functools.partial(step_kernel, row_devices, col_devices),...  82 us
    pallas_call x1, Pallas kernels, body(): pl.pallas_call(place_kernel, out_shape=shapes, in_specs=[anywhere] * 5, o...  2.85 us

profile of v4, /device:TPU:0, one launch (start us, length us, event | category | flops | bytes accessed | tf_op | source)
XLA Modules:
  0.0 85.4 jit_solution(1131536441700772138)
XLA Ops:
  0.6 82.0 %panel_step.1 = (f32[64,2048]{1,0:T(8,128)}, f32[256,256]{1,0:T(8,128)}, f32[256,256]{1,0:T(8,128)}, f32[2048,256]{1,0:T(8,128)}, f32[64,256]{1,0:T(8,128)}) custom-call(f32[64,2048]{1,0:T(8,128)} %panel_hbm.1, f32[2048,256]{1,0:T(8,128)} %trailing_hbm.1, f32[64,2048]{1,0:T(8,128)} %prev_hbm.1, f32[256,256]{1,0:T(8,128)} %prev_upper_hbm.1, ...), custom_call_target="tpu_custom_call" | custom-call | tf_op jit(solution)/shard_map/panel_step/pallas_call | solution.py:528
  82.6 2.8 %place_outputs.1 = (f32[64,2048]{1,0:T(8,128)}, f32[256,256]{1,0:T(8,128)}, f32[256,256]{1,0:T(8,128)}, f32[2048,256]{1,0:T(8,128)}, f32[64,256]{1,0:T(8,128)}) custom-call(f32[64,2048]{1,0:T(8,128)} %get-tuple-element.10.refs_0_, f32[256,256]{1,0:T(8,128)} %get-tuple-element.11.refs_1_, f32[256,256]{1,0:T(8,128)} %get-tuple-element.12.refs_2_, ...), custom_call_target="tpu_custom_call" | custom-call | tf_op jit(solution)/shard_map/place_outputs/pallas_call | solution.py:571

commit v5 on v4

--- a/solution.py
+++ b/solution.py
@@ -361,10 +361,12 @@
         total = total + picked_in[d]
     block[own_row, own_col] = total
     start_all(zone_copy, col_devices)
+    for q in range(HALF, HALF + 2):
+        step(0, q)
     land_all(zone_copy, col_devices)
     start_all(block_copy, row_devices)
     start_all(trail_copy, row_devices)
-    for q in range(HALF, PIECES):
+    for q in range(HALF + 2, PIECES):
         step(0, q)
     land_all(block_copy, row_devices)
 
@@ -379,12 +381,20 @@
     x[...] = matrix.T
 
     count = order // BLOCK
+    early = PIECES // (count // 2)
 
     @pl.loop(0, count)
     def _(stage):
         lu_stage(stage, order, w, x, u_ref, linv, uinvt)
-        for part in range(PIECES // count):
-            step(1, stage * (PIECES // count) + part)
+
+        @pl.when(stage < count // 2)
+        def _():
+            for part in range(early):
+                step(1, stage * early + part)
+
+        @pl.when(stage >= count // 2)
+        def _():
+            step(2, stage - count // 2)
 
         @pl.when(stage == 2)
         def _():
@@ -406,7 +416,7 @@
     right_copy.start()
     for hop in range(2, col_devices - 1):
 
-        @pl.loop(0, PIECES)
+        @pl.loop(count // 2 if hop == 2 else 0, PIECES)
         def _(q):
             step(hop, q)
 
@@ -436,7 +446,8 @@
 
         trailing_ref[here, :] = trailing_ref[here, :] - product(lower, right_ref[...], 0, 0)
 
-    last = pltpu.make_async_copy(gram_ref, gram_hbm, out_sem.at[2])
+    def last_copy():
+        return pltpu.make_async_copy(gram_ref, gram_hbm, out_sem.at[2])
 
     @pl.loop(0, HALF)
     def _(q):
@@ -447,7 +458,7 @@
             for d in range(1, row_devices):
                 total = total + gram_in[d]
             gram_ref[...] = total / (rows_here * row_devices)
-            last.start()
+            last_copy().start()
 
         step(col_devices - 1, q + HALF)
         here = pl.ds(pl.multiple_of(q * span, span), span)
@@ -484,7 +495,7 @@
 
     u_copy.wait()
     right_copy.wait()
-    last.wait()
+    last_copy().wait()
 
 
 def place_kernel(*refs):

time: 85.6 us -> 84.4 us (0.986)
  Pallas kernels: 84.8 us -> 83.6 us
    pallas_call x1, Pallas kernels: 82 us -> 80.7 us  [body(): pl.pallas_call(functools.partial(step_kernel, row_devices, col_devices),...]
where the time goes in v5:
time: 84.4 us; the launch traced here: 84.2 us
  Pallas kernels  83.6 us (99%)
    pallas_call x1, Pallas kernels, body(): pl.pallas_call(functools.partial(step_kernel, row_devices, col_devices),...  80.7 us
    pallas_call x1, Pallas kernels, body(): pl.pallas_call(place_kernel, out_shape=shapes, in_specs=[anywhere] * 5, o...  2.85 us

profile of v5, /device:TPU:0, one launch (start us, length us, event | category | flops | bytes accessed | tf_op | source)
XLA Modules:
  0.0 84.2 jit_solution(3732885840945161298)
XLA Ops:
  0.6 80.7 %panel_step.1 = (f32[64,2048]{1,0:T(8,128)}, f32[256,256]{1,0:T(8,128)}, f32[256,256]{1,0:T(8,128)}, f32[2048,256]{1,0:T(8,128)}, f32[64,256]{1,0:T(8,128)}) custom-call(f32[64,2048]{1,0:T(8,128)} %panel_hbm.1, f32[2048,256]{1,0:T(8,128)} %trailing_hbm.1, f32[64,2048]{1,0:T(8,128)} %prev_hbm.1, f32[256,256]{1,0:T(8,128)} %prev_upper_hbm.1, ...), custom_call_target="tpu_custom_call" | custom-call | tf_op jit(solution)/shard_map/panel_step/pallas_call | solution.py:539
  81.4 2.8 %place_outputs.1 = (f32[64,2048]{1,0:T(8,128)}, f32[256,256]{1,0:T(8,128)}, f32[256,256]{1,0:T(8,128)}, f32[2048,256]{1,0:T(8,128)}, f32[64,256]{1,0:T(8,128)}) custom-call(f32[64,2048]{1,0:T(8,128)} %get-tuple-element.10.refs_0_, f32[256,256]{1,0:T(8,128)} %get-tuple-element.11.refs_1_, f32[256,256]{1,0:T(8,128)} %get-tuple-element.12.refs_2_, ...), custom_call_target="tpu_custom_call" | custom-call | tf_op jit(solution)/shard_map/place_outputs/pallas_call | solution.py:582

commit v6 on v5

--- a/solution.py
+++ b/solution.py
@@ -230,8 +230,6 @@
     ]
     for copy in loads[:2] + own_copies + loads[2:]:
         copy.start()
-    for copy in own_copies:
-        copy.wait()
     pl.semaphore_wait(barrier, row_devices + col_devices - 2)
 
     def tall_copy(q, source, way, to):
@@ -245,9 +243,8 @@
             device_id_type=MESH,
         )
 
-    def step(hop, q):
+    def step_up(hop, q):
         up = own_col - hop
-        down = own_col + hop
         if hop > 0:
 
             @pl.when(up >= 0)
@@ -258,6 +255,8 @@
         def _():
             tall_copy(q, up, 0, own_col + 1).start()
 
+    def step_down(hop, q):
+        down = own_col + hop
         if hop > 0:
 
             @pl.when(down < col_devices)
@@ -267,6 +266,17 @@
         @pl.when((down < col_devices) & (own_col > 0))
         def _():
             tall_copy(q, down, 1, own_col - 1).start()
+
+    def step(hop, q):
+        @pl.when(own_col < col_devices // 2)
+        def _():
+            step_down(hop, q)
+            step_up(hop, q)
+
+        @pl.when(own_col >= col_devices // 2)
+        def _():
+            step_up(hop, q)
+            step_down(hop, q)
 
     def share_of(d):
         return pl.ds(pl.multiple_of(lax.rem(own_row + d, row_devices) * share, share), share)
@@ -322,7 +332,10 @@
             copy(d).wait_send()
 
     for q in range(HALF):
+        own_copies[q].wait()
         step(0, q)
+    for copy in own_copies[HALF:]:
+        copy.wait()
     loads[0].wait()
     loads[1].wait()
     target = trace_rows(merge_ref, leaf_ref, row_devices, own_row)

time: 84.4 us -> 84.1 us (level)
  no operation moved by 1% of the time
where the time goes in v6:
time: 84.1 us; the launch traced here: 83.9 us
  Pallas kernels  83.3 us (99%)
    pallas_call x1, Pallas kernels, body(): pl.pallas_call(functools.partial(step_kernel, row_devices, col_devices),...  80.5 us
    pallas_call x1, Pallas kernels, body(): pl.pallas_call(place_kernel, out_shape=shapes, in_specs=[anywhere] * 5, o...  2.85 us

profile of v6, /device:TPU:0, one launch (start us, length us, event | category | flops | bytes accessed | tf_op | source)
XLA Modules:
  0.0 83.9 jit_solution(17537467524515322097)
XLA Ops:
  0.6 80.5 %panel_step.1 = (f32[64,2048]{1,0:T(8,128)}, f32[256,256]{1,0:T(8,128)}, f32[256,256]{1,0:T(8,128)}, f32[2048,256]{1,0:T(8,128)}, f32[64,256]{1,0:T(8,128)}) custom-call(f32[64,2048]{1,0:T(8,128)} %panel_hbm.1, f32[2048,256]{1,0:T(8,128)} %trailing_hbm.1, f32[64,2048]{1,0:T(8,128)} %prev_hbm.1, f32[256,256]{1,0:T(8,128)} %prev_upper_hbm.1, ...), custom_call_target="tpu_custom_call" | custom-call | tf_op jit(solution)/shard_map/panel_step/pallas_call | solution.py:552
  81.1 2.8 %place_outputs.1 = (f32[64,2048]{1,0:T(8,128)}, f32[256,256]{1,0:T(8,128)}, f32[256,256]{1,0:T(8,128)}, f32[2048,256]{1,0:T(8,128)}, f32[64,256]{1,0:T(8,128)}) custom-call(f32[64,2048]{1,0:T(8,128)} %get-tuple-element.10.refs_0_, f32[256,256]{1,0:T(8,128)} %get-tuple-element.11.refs_1_, f32[256,256]{1,0:T(8,128)} %get-tuple-element.12.refs_2_, ...), custom_call_target="tpu_custom_call" | custom-call | tf_op jit(solution)/shard_map/place_outputs/pallas_call | solution.py:595
